TPU v7x, 128 devices: a whole 4x4x4 slice. The times are simulated.
128 devices in a mesh: rows: 2 (over core), cols: 64 (over z, y, x).
Axes of the slice: x: 4, y: 4, z: 4, core: 2. Of those that a mesh axis runs over, the one named last changes fastest.
Arguments:
- row_geom: float32 [3072, 8, 1024], P('cols', None, 'rows'), may hold values from -1 to 1
- col_geom: float32 [3072, 8, 1024], P('cols', None, 'rows'), may hold values from -1 to 1
- row_start: int32 [3072], P('cols'), may hold values from 1024 to 397951
- col_start: int32 [3072], P('cols'), may hold values from 512 to 398463, as said below
- block_count: int32 [64], P('cols'), may hold values from 1 to 48, 768 in all
- sketch: float32 [1024, 64], replicated, may hold values from -0.75 to 0.75
Outputs:
- left_factor: float32 [3072, 64, 1024], P('cols', None, 'rows')
- right_factor: float32 [3072, 64, 1024], P('cols', None, 'rows')
Inputs may be any that keep to these rules, and one draw needn't show every extreme that they name: `block_count`: each owner's counts are at most 48; all counts together sum to exactly 48 // 4 times the number of owners. Places beyond an owner's count are unused. col_start minus row_start lies between -512 and 512.
All inputs are finite; a program needn't handle non-finite values. No bound on the sum of `block_count` on one device may be relied on, other than what follows from the above.
Results may differ from a plain program's by a relative error of at most 0.0003.
Values sent between devices are 32-bit elements; how exact they have to be, the bound alone decides.
A program may use at most 128 MiB of HBM per device.

v0:
```python
import jax
import jax.numpy as jnp
from jax import lax
from jax.sharding import PartitionSpec as P

HIGHEST = lax.Precision.HIGHEST


def copy_for_each(shard, axis):
    copies = jnp.broadcast_to(shard, (lax.axis_size(axis), *shard.shape))
    return lax.all_to_all(copies, axis, split_axis=0, concat_axis=0, tiled=True)


def combined_pairwise(pieces, combine):
    while len(jax.tree.leaves(pieces)[0]) > 1:
        pieces = jax.vmap(combine)(*(pieces[side::2] for side in (0, 1)))
    return pieces[0]


def carried_in(shard, axis, combine, identity):
    count, here = (lax.axis_size(axis), lax.axis_index(axis))
    passed = jnp.arange(count) < here

    def kept(part, zero, own):
        part = jnp.where(
            passed.reshape(-1, *(1 for _ in own.shape)), part, jnp.asarray(zero, own.dtype)
        )
        return part

    pieces = copy_for_each(shard, axis)
    return combined_pairwise(kept(pieces, identity, shard), combine)


def kernel_block(row_geo, col_geo, start_row, start_col):
    sep_x = row_geo[:, 0, :, None] - col_geo[:, 0, None, :]
    sep_y = row_geo[:, 1, :, None] - col_geo[:, 1, None, :]
    sep_z = row_geo[:, 2, :, None] - col_geo[:, 2, None, :]
    row_area = 0.1 + 0.05 * row_geo[:, 6, :, None]
    col_area = 0.1 + 0.05 * col_geo[:, 6, None, :]
    inverse = 1.0 / (sep_x * sep_x + sep_y * sep_y + sep_z * sep_z + row_area + col_area)
    normal_dot = (
        row_geo[:, 3, :, None] * col_geo[:, 3, None, :]
        + row_geo[:, 4, :, None] * col_geo[:, 4, None, :]
        + row_geo[:, 5, :, None] * col_geo[:, 5, None, :]
    )
    row_proj = (
        row_geo[:, 3, :, None] * sep_x
        + row_geo[:, 4, :, None] * sep_y
        + row_geo[:, 5, :, None] * sep_z
    )
    col_proj = (
        col_geo[:, 3, None, :] * sep_x
        + col_geo[:, 4, None, :] * sep_y
        + col_geo[:, 5, None, :] * sep_z
    )
    influence = (
        col_area * (normal_dot - 3.0 * row_proj * col_proj * inverse) * inverse * jnp.sqrt(inverse)
    )
    self_term = 4.0 + 2.0 * row_geo[:, 7, :, None]
    row_ids = jnp.arange(row_geo.shape[2], dtype=jnp.int32)[:, None]
    col_ids = jnp.arange(col_geo.shape[2], dtype=jnp.int32)[None, :]
    distance = (start_row - start_col)[:, None, None]
    match = (col_ids - row_ids)[None, :, :] == distance
    return jnp.where(match, self_term, influence)


def factor_pair(gram, projected):
    rank = gram.shape[1]
    trace = jnp.trace(gram, axis1=1, axis2=2)
    ridge = 0.01 * trace / rank + 0.001
    system = gram + ridge[:, None, None] * jnp.eye(rank, dtype=gram.dtype)[None]
    lower = jnp.linalg.cholesky(system)
    half = lax.linalg.triangular_solve(lower, projected, left_side=True, lower=True)
    return lax.linalg.triangular_solve(lower, half, left_side=True, lower=True, transpose_a=True)


def pick_group(total, most):
    group = most
    while total % group:
        group -= 1
    return group


def add_counts(earlier, later):
    return earlier + later


def whole_compress(row_geo, col_geo, row_start, col_start, sketch):
    slots, geo_count, width = row_geo.shape
    rank = sketch.shape[1]
    ranks = lax.axis_size("rows")
    my_index = lax.axis_index("rows")
    turns = slots // ranks
    stacked = jnp.stack([row_geo, col_geo], 1).reshape(turns, ranks, 2, geo_count, width)
    gathered = lax.all_to_all(stacked, "rows", split_axis=1, concat_axis=4, tiled=True)
    full_width = gathered.shape[4]
    full_rows = gathered[:, 0, 0]
    full_cols = gathered[:, 0, 1]
    my_row_start = lax.dynamic_index_in_dim(
        row_start.reshape(turns, ranks), my_index, 1, keepdims=False
    )
    my_col_start = lax.dynamic_index_in_dim(
        col_start.reshape(turns, ranks), my_index, 1, keepdims=False
    )
    group = pick_group(turns, 2)
    batches = turns // group

    def step(carry, packed):
        rows_part, cols_part, first_row, first_col = packed
        block = kernel_block(rows_part, cols_part, first_row, first_col)
        sketched = jnp.einsum("gik,kr->gir", block, sketch, precision=HIGHEST)
        gram = jnp.einsum("gir,gis->grs", sketched, sketched, precision=HIGHEST)
        projected = jnp.einsum("gik,gir->grk", block, sketched, precision=HIGHEST)
        right = factor_pair(gram, projected)
        left = jnp.transpose(sketched, (0, 2, 1))
        return (carry, jnp.stack([left, right], 1))

    packed = (
        full_rows.reshape(batches, group, geo_count, full_width),
        full_cols.reshape(batches, group, geo_count, full_width),
        my_row_start.reshape(batches, group),
        my_col_start.reshape(batches, group),
    )
    results = lax.scan(step, jnp.int32(0), packed)[1]
    results = results.reshape(turns, 1, 2, rank, full_width)
    returned = lax.all_to_all(results, "rows", split_axis=4, concat_axis=1, tiled=True)
    flat = returned.reshape(slots, 2, rank, width)
    return (flat[:, 0], flat[:, 1])


def compress(row_geo, col_geo, row_start, col_start, sketch):
    return whole_compress(row_geo, col_geo, row_start, col_start, sketch)


def on_device(row_geom, col_geom, row_start, col_start, block_count, sketch):
    owned, geo_count, width = row_geom.shape
    rank = sketch.shape[1]
    count = block_count[0]
    order = jnp.arange(owned, dtype=jnp.int32)
    owners = lax.axis_size("cols")
    capacity = -(-owned // owners)
    total_slots = owners * capacity
    start = carried_in(count, "cols", add_counts, jnp.int32(0))
    workers = jnp.arange(owners, dtype=jnp.int32)[:, None]
    places = jnp.arange(capacity, dtype=jnp.int32)[None, :]
    picked = places * owners + (workers - start) % owners
    is_sent = picked < count
    safe = jnp.minimum(picked, owned - 1)
    send_rows = jnp.where(is_sent[:, :, None, None], row_geom[safe], 0.0)
    send_cols = jnp.where(is_sent[:, :, None, None], col_geom[safe], 0.0)
    send_ranges = jnp.stack(
        [
            jnp.where(is_sent, row_start[safe], 0),
            jnp.where(is_sent, col_start[safe], 0),
            jnp.where(is_sent, start + picked, -1),
        ],
        2,
    ).astype(jnp.float32)
    got_rows, got_cols, got_ranges = (
        lax.all_to_all(send_rows, "cols", split_axis=0, concat_axis=0, tiled=True),
        lax.all_to_all(send_cols, "cols", split_axis=0, concat_axis=0, tiled=True),
        lax.all_to_all(send_ranges, "cols", split_axis=0, concat_axis=0, tiled=True),
    )
    ranges = got_ranges.reshape(total_slots, 3).astype(jnp.int32)
    busy = owned // 4
    flat_ids = ranges[:, 2]
    is_live = flat_ids >= 0
    target = jnp.where(is_live, flat_ids // owners, busy)
    chosen = target[None, :] == jnp.arange(busy, dtype=jnp.int32)[:, None]
    source = jnp.sum(
        jnp.where(chosen, jnp.arange(total_slots, dtype=jnp.int32)[None, :], 0), axis=1
    )
    busy_rows = got_rows.reshape(total_slots, geo_count, width)[source]
    busy_cols = got_cols.reshape(total_slots, geo_count, width)[source]
    left_busy, right_busy = compress(
        busy_rows, busy_cols, ranges[source, 0], ranges[source, 1], sketch
    )
    slot_pick = jnp.minimum(target, busy - 1)
    back_left = jnp.where(is_live[:, None, None], left_busy[slot_pick], 0.0).reshape(
        owners, capacity, rank, width
    )
    back_right = jnp.where(is_live[:, None, None], right_busy[slot_pick], 0.0).reshape(
        owners, capacity, rank, width
    )
    returned_left, returned_right = (
        lax.all_to_all(back_left, "cols", split_axis=0, concat_axis=0, tiled=True),
        lax.all_to_all(back_right, "cols", split_axis=0, concat_axis=0, tiled=True),
    )
    flat_index = (start + order) % owners * capacity + order // owners
    left = returned_left.reshape(total_slots, rank, width)[flat_index]
    right = returned_right.reshape(total_slots, rank, width)[flat_index]
    is_kept = (order < count)[:, None, None]
    return (jnp.where(is_kept, left, 0.0), jnp.where(is_kept, right, 0.0))


def solution(mesh):
    placed = (
        P("cols", None, "rows"),
        P("cols", None, "rows"),
        P("cols"),
        P("cols"),
        P("cols"),
        P(),
    )
    return jax.shard_map(
        on_device,
        mesh=mesh,
        in_specs=placed,
        out_specs=(P("cols", None, "rows"), P("cols", None, "rows")),
        check_vma=False,
    )
```

profile of v0, /device:TPU:4, one launch (start us, length us, event | category | flops | bytes accessed | tf_op | source)
XLA Modules:
  0.0 634.6 jit_solution(12272790962720469400)
XLA Ops:
  2.0 11.5 %all-to-all-start = ((s32[64,1,1]{2,1,0:T(1,128)}), s32[64,1,1]{2,1,0:T(1,128)S(1)}, u32[]{:S(2)}, u32[]{:S(2)}) async-start(s32[64,1,1]{2,1,0:T(1,128)} %broadcast_in_dim.145), calls=%async_computation | async-start | bytes 65536 | tf_op jit(solution)/shard_map/all_to_all | solution.py:11
  13.5 7.5 %all-to-all-done = s32[64,1,1]{2,1,0:T(1,128)S(1)} async-done(((s32[64,1,1]{2,1,0:T(1,128)}), s32[64,1,1]{2,1,0:T(1,128)S(1)}, u32[]{:S(2)}, u32[]{:S(2)}) %all-to-all-start) | async-done | bytes 288 | tf_op jit(solution)/shard_map/all_to_all | solution.py:11
  21.0 1.2 reduce.12
  25.2 1.4 gather_fusion
  26.7 1.4 gather_fusion.1
  28.9 6.9 %all-to-all-start.1 = ((f32[64,1,3]{2,1,0:T(1,128)}), f32[64,1,3]{2,1,0:T(1,128)S(1)}, u32[]{:S(2)}, u32[]{:S(2)}) async-start(f32[64,1,3]{2,1,0:T(1,128)} %copy.46), calls=%async_computation.1 | async-start | bytes 65536 | tf_op jit(solution)/shard_map/all_to_all | solution.py:162
  36.5 1.8 gather_fusion.6
  38.3 5.0 all-to-all-done.1
  44.0 1.2 bitcast_select_fusion.3
  45.2 20.9 %all_to_all.67 = f32[64,1,8,512]{3,2,1,0:T(8,128)S(1)} all-to-all(f32[64,1,8,512]{3,2,1,0:T(8,128)S(1)} %get-tuple-element.163), channel_id=1, replica_groups=mesh['rows'=2,'cols'=64] {'cols'}, dimensions={0} | all-to-all | bytes 2097152 | tf_op jit(solution)/shard_map/all_to_all | solution.py:160
  66.1 6.4 %all-to-all-start.3 = ((f32[64,1,8,512]{3,2,1,0:T(8,128)}), f32[64,1,8,512]{3,2,1,0:T(8,128)S(1)}, u32[]{:S(2)}, u32[]{:S(2)}) async-start(f32[64,1,8,512]{3,2,1,0:T(8,128)} %get-tuple-element.164), calls=%async_computation.3 | async-start | bytes 2097152 | tf_op jit(solution)/shard_map/all_to_all | solution.py:161
  72.7 0.7 gather_fusion.2
  73.5 0.7 gather_fusion.3
  75.9 10.3 %all-to-all-done.3 = f32[64,1,8,512]{3,2,1,0:T(8,128)S(1)} async-done(((f32[64,1,8,512]{3,2,1,0:T(8,128)}), f32[64,1,8,512]{3,2,1,0:T(8,128)S(1)}, u32[]{:S(2)}, u32[]{:S(2)}) %all-to-all-start.3) | async-done | bytes 1048608 | tf_op jit(solution)/shard_map/all_to_all | solution.py:161
  86.8 4.0 all_to_all.68
  90.9 208.2 %while.12 = (s32[]{:T(128)}, f32[3,2,2,64,1024]{4,3,2,1,0:T(8,128)}, s32[3,2]{1,0:T(4,128)S(1)}, s32[3,2]{1,0:T(4,128)S(1)}, f32[3,2,8,1024]{3,2,1,0:T(8,128)S(1...) while((s32[]{:T(128)}, f32[3,2,2,64,1024]{4,3,2,1,0:T(8,128)}, ...), condition=%wide.region_5.6_spmd, body=%wide.region_1.5_spmd.sunk | while | flops 3671470336 | bytes 37377732 | solution.py:124
  92.0 21.5 %fusion.96 = f32[2,1024,64]{1,2,0:T(8,128)S(1)} fusion(f32[2,1024]{1,0:T(2,128)S(1)} %get-tuple-element.239, f32[2,1024]{1,0:T(2,128)S(1)} %get-tuple-element.241, f32[2,1024]{1,0:T(2,128)S(1)} %get-tuple-element.242, f32[2,1024]{1,0:T(2,128)S(1)} %get-tuple-element.243, f32[2,1024]{1,0:T(2,128)S(1)} %get-tuple-element.244, ...), kind=kOutput, calls=%fused_computation.40.clone.1 | convolution fusion | flops 1684013056 | bytes 5103624 | tf_op jit(solution)/shard_map/while/body/eval_jaxpr/gik,kr->gir/dot_general | solution.py:111
  114.4 11.7 %custom-call.42 = f32[2,64,64]{2,1,0:T(8,128)S(1)} custom-call(f32[2,64,64]{2,1,0:T(8,128)S(1)} %fusion.99), custom_call_target="Cholesky" | custom-call | tf_op jit(solution)/shard_map/while/body/eval_jaxpr/jit(cholesky)/cholesky | solution.py:72
  126.4 10.0 %custom-call.43 = f32[2,1,64,64]{2,3,1,0:T(8,128)S(1)} custom-call(f32[2,1,64,64]{3,2,1,0:T(8,128)S(1)} %select_bitcast_fusion.3), custom_call_target="InvertDiagBlocksLowerTriangular" | custom-call | tf_op jit(solution)/shard_map/while/body/eval_jaxpr/triangular_solve | solution.py:74
  136.4 20.7 %fusion.97 = f32[2,64,1024]{2,1,0:T(8,128)S(1)} fusion(f32[2,1024,64]{1,2,0:T(8,128)S(1)} %fusion.96, f32[2,1024]{1,0:T(2,128)S(1)} %get-tuple-element.239, f32[2,1024]{1,0:T(2,128)S(1)} %get-tuple-element.241, f32[2,1024]{1,0:T(2,128)S(1)} %get-tuple-element.242, f32[2,1024]{1,0:T(2,128)S(1)} %get-tuple-element.243, ...), kind=kOutput, calls=%fused_computation.39.clone.1 | convolution fusion | flops 1684013056 | bytes 5365768 | tf_op jit(solution)/shard_map/while/body/eval_jaxpr/gik,gir->grk/dot_general | solution.py:113
  158.2 1.1 copy_dynamic-update-slice_fusion.2
  160.5 21.1 %fusion.96 = f32[2,1024,64]{1,2,0:T(8,128)S(1)} fusion(f32[2,1024]{1,0:T(2,128)S(1)} %get-tuple-element.239, f32[2,1024]{1,0:T(2,128)S(1)} %get-tuple-element.241, f32[2,1024]{1,0:T(2,128)S(1)} %get-tuple-element.242, f32[2,1024]{1,0:T(2,128)S(1)} %get-tuple-element.243, f32[2,1024]{1,0:T(2,128)S(1)} %get-tuple-element.244, ...), kind=kOutput, calls=%fused_computation.40.clone.1 | convolution fusion | flops 1684013056 | bytes 5103624 | tf_op jit(solution)/shard_map/while/body/eval_jaxpr/gik,kr->gir/dot_general | solution.py:111
  182.5 11.7 %custom-call.42 = f32[2,64,64]{2,1,0:T(8,128)S(1)} custom-call(f32[2,64,64]{2,1,0:T(8,128)S(1)} %fusion.99), custom_call_target="Cholesky" | custom-call | tf_op jit(solution)/shard_map/while/body/eval_jaxpr/jit(cholesky)/cholesky | solution.py:72
  194.5 10.0 %custom-call.43 = f32[2,1,64,64]{2,3,1,0:T(8,128)S(1)} custom-call(f32[2,1,64,64]{3,2,1,0:T(8,128)S(1)} %select_bitcast_fusion.3), custom_call_target="InvertDiagBlocksLowerTriangular" | custom-call | tf_op jit(solution)/shard_map/while/body/eval_jaxpr/triangular_solve | solution.py:74
  204.6 20.8 %fusion.97 = f32[2,64,1024]{2,1,0:T(8,128)S(1)} fusion(f32[2,1024,64]{1,2,0:T(8,128)S(1)} %fusion.96, f32[2,1024]{1,0:T(2,128)S(1)} %get-tuple-element.239, f32[2,1024]{1,0:T(2,128)S(1)} %get-tuple-element.241, f32[2,1024]{1,0:T(2,128)S(1)} %get-tuple-element.242, f32[2,1024]{1,0:T(2,128)S(1)} %get-tuple-element.243, ...), kind=kOutput, calls=%fused_computation.39.clone.1 | convolution fusion | flops 1684013056 | bytes 5365768 | tf_op jit(solution)/shard_map/while/body/eval_jaxpr/gik,gir->grk/dot_general | solution.py:113
  226.6 1.1 copy_dynamic-update-slice_fusion.2
  228.6 21.1 %fusion.96 = f32[2,1024,64]{1,2,0:T(8,128)S(1)} fusion(f32[2,1024]{1,0:T(2,128)S(1)} %get-tuple-element.239, f32[2,1024]{1,0:T(2,128)S(1)} %get-tuple-element.241, f32[2,1024]{1,0:T(2,128)S(1)} %get-tuple-element.242, f32[2,1024]{1,0:T(2,128)S(1)} %get-tuple-element.243, f32[2,1024]{1,0:T(2,128)S(1)} %get-tuple-element.244, ...), kind=kOutput, calls=%fused_computation.40.clone.1 | convolution fusion | flops 1684013056 | bytes 5103624 | tf_op jit(solution)/shard_map/while/body/eval_jaxpr/gik,kr->gir/dot_general | solution.py:111
  250.7 11.7 %custom-call.42 = f32[2,64,64]{2,1,0:T(8,128)S(1)} custom-call(f32[2,64,64]{2,1,0:T(8,128)S(1)} %fusion.99), custom_call_target="Cholesky" | custom-call | tf_op jit(solution)/shard_map/while/body/eval_jaxpr/jit(cholesky)/cholesky | solution.py:72
  262.7 10.2 %custom-call.43 = f32[2,1,64,64]{2,3,1,0:T(8,128)S(1)} custom-call(f32[2,1,64,64]{3,2,1,0:T(8,128)S(1)} %select_bitcast_fusion.3), custom_call_target="InvertDiagBlocksLowerTriangular" | custom-call | tf_op jit(solution)/shard_map/while/body/eval_jaxpr/triangular_solve | solution.py:74
  272.9 20.6 %fusion.97 = f32[2,64,1024]{2,1,0:T(8,128)S(1)} fusion(f32[2,1024,64]{1,2,0:T(8,128)S(1)} %fusion.96, f32[2,1024]{1,0:T(2,128)S(1)} %get-tuple-element.239, f32[2,1024]{1,0:T(2,128)S(1)} %get-tuple-element.241, f32[2,1024]{1,0:T(2,128)S(1)} %get-tuple-element.242, f32[2,1024]{1,0:T(2,128)S(1)} %get-tuple-element.243, ...), kind=kOutput, calls=%fused_computation.39.clone.1 | convolution fusion | flops 1684013056 | bytes 5365768 | tf_op jit(solution)/shard_map/while/body/eval_jaxpr/gik,gir->grk/dot_general | solution.py:113
  294.7 1.1 copy_dynamic-update-slice_fusion.2
  299.1 9.4 %copy.54 = f32[6,1,2,64,1024]{3,2,0,1,4:T(2,128)} copy(f32[6,1,2,64,1024]{4,3,2,0,1:T(8,128)} %bitcast.50) | data formatting | bytes 6291456 | tf_op jit(solution)/shard_map/reshape | solution.py:125
  308.5 9.6 %reshape.618 = f32[2,1,393216]{2,1,0:T(1,128)} reshape(f32[1024,1,6,2,64]{4,3,2,1,0:T(2,128)} %bitcast.201) | data formatting | bytes 6291456
  318.1 10.8 %all_to_all.69 = f32[2,1,393216]{2,1,0:T(1,128)} all-to-all(f32[2,1,393216]{2,1,0:T(1,128)} %reshape.618), channel_id=1, replica_groups=mesh['rows'=2,'cols'=64] {'rows'}, dimensions={0} | all-to-all | bytes 6291456 | tf_op jit(solution)/shard_map/all_to_all | solution.py:126
  329.4 12.6 %reduce.17 = f32[2,393216]{1,0:T(2,128)} reduce(f32[2,1,393216]{2,1,0:T(1,128)} %all_to_all.69, f32[]{:T(128)} %broadcast.1032), dimensions={1}, to_apply=%all_to_all.54.reduce_sub_computation | reduce | bytes 6291460 | tf_op jit(solution)/shard_map/all_to_all | solution.py:126
  342.0 10.4 %reshape.619 = f32[1024,1,6,2,64]{4,3,2,1,0:T(2,128)} reshape(f32[2,393216]{1,0:T(2,128)} %reduce.17) | data formatting | bytes 6291456
  352.3 9.4 %copy.61 = f32[6,1,2,64,2,512]{5,4,3,2,0,1:T(2,128)} copy(f32[6,1,2,64,2,512]{3,2,0,5,4,1:T(2,128)} %bitcast.202) | data formatting | bytes 6291456 | tf_op jit(solution)/shard_map/all_to_all | solution.py:126
  361.8 2.5 copy.56
  364.3 1.4 slice_bitcast_fusion.12
  365.7 5.8 gather_fusion.8
  371.5 4.6 gather_fusion.10
  376.1 9.4 %fusion.41 = (f32[64,1,64,512]{3,2,1,0:T(8,128)}, f32[64,1,64,512]{3,2,1,0:T(8,128)S(1)}) fusion(f32[64,64,512]{2,1,0:T(8,128)} %gather_fusion.10, pred[64]{0:T(512)(128)(4,1)S(1)} %copy-done.3, f32[64,64,512]{2,1,0:T(8,128)} %gather_fusion.8), kind=kLoop, calls=%fused_computation.95 | loop fusion | flops 4194304 | bytes 33554496 | tf_op jit(solution)/shard_map/jit(_where)/select_n | solution.py:182
  385.5 102.9 %all_to_all.70 = f32[64,1,64,512]{3,2,1,0:T(8,128)} all-to-all(f32[64,1,64,512]{3,2,1,0:T(8,128)S(1)} %get-tuple-element.162), channel_id=1, replica_groups=mesh['rows'=2,'cols'=64] {'cols'}, dimensions={0} | all-to-all | bytes 16777216 | tf_op jit(solution)/shard_map/all_to_all | solution.py:186
  488.4 7.9 %all-to-all-start.7 = ((f32[64,1,64,512]{3,2,1,0:T(8,128)}), f32[64,1,64,512]{3,2,1,0:T(8,128)}, u32[]{:S(2)}, u32[]{:S(2)}) async-start(f32[64,1,64,512]{3,2,1,0:T(8,128)} %get-tuple-element.161), calls=%async_computation.7 | async-start | bytes 16777216 | tf_op jit(solution)/shard_map/all_to_all | solution.py:187
  496.4 7.0 %gather_fusion.9 = f32[48,64,512]{2,1,0:T(8,128)} fusion(f32[64,64,512]{2,1,0:T(8,128)} %bitcast.200, s32[1024]{0:T(1024)S(1)} %pad_clamp_fusion), kind=kCustom, calls=%fused_computation.9 | custom fusion | bytes 12583104 | tf_op jit(solution)/shard_map/gather | solution.py:190
  503.4 111.5 %all-to-all-done.7 = f32[64,1,64,512]{3,2,1,0:T(8,128)} async-done(((f32[64,1,64,512]{3,2,1,0:T(8,128)}), f32[64,1,64,512]{3,2,1,0:T(8,128)}, u32[]{:S(2)}, u32[]{:S(2)}) %all-to-all-start.7) | async-done | bytes 8388640 | tf_op jit(solution)/shard_map/all_to_all | solution.py:187
  614.9 7.1 %gather_fusion.11 = f32[48,64,512]{2,1,0:T(8,128)} fusion(f32[64,64,512]{2,1,0:T(8,128)} %bitcast.63, s32[1024]{0:T(1024)S(1)} %pad_clamp_fusion), kind=kCustom, calls=%fused_computation.11 | custom fusion | bytes 12583104 | tf_op jit(solution)/shard_map/gather | solution.py:191
  622.0 12.4 %broadcast_select_fusion = (f32[48,64,512]{2,1,0:T(8,128)}, f32[48,64,512]{2,1,0:T(8,128)}) fusion(f32[48,64,512]{2,1,0:T(8,128)} %gather_fusion.11, pred[48]{0:T(512)(128)(4,1)S(1)} %iota_compare_fusion.4, f32[48,64,512]{2,1,0:T(8,128)} %gather_fusion.9), kind=kLoop, calls=%fused_computation.98 | loop fusion | flops 3145728 | bytes 25165872 | tf_op jit(solution)/shard_map/jit(_where)/select_n | solution.py:193
  (122 shorter events, 16.6 us)
Async XLA Ops:
  0.6 35.2 %copy-start = (f32[48,8,512]{2,1,0:T(8,128)S(1)}, f32[48,8,512]{2,1,0:T(8,128)}, u32[]{:S(2)}) copy-start(f32[48,8,512]{2,1,0:T(8,128)} %param.8) | copy-start | bytes 2359300
  2.0 19.0 %all-to-all-start = ((s32[64,1,1]{2,1,0:T(1,128)}), s32[64,1,1]{2,1,0:T(1,128)S(1)}, u32[]{:S(2)}, u32[]{:S(2)}) async-start(s32[64,1,1]{2,1,0:T(1,128)} %broadcast_in_dim.145), calls=%async_computation | async-start | bytes 65536 | tf_op jit(solution)/shard_map/all_to_all | solution.py:11
  28.9 14.4 %all-to-all-start.1 = ((f32[64,1,3]{2,1,0:T(1,128)}), f32[64,1,3]{2,1,0:T(1,128)S(1)}, u32[]{:S(2)}, u32[]{:S(2)}) async-start(f32[64,1,3]{2,1,0:T(1,128)} %copy.46), calls=%async_computation.1 | async-start | bytes 65536 | tf_op jit(solution)/shard_map/all_to_all | solution.py:162
  36.5 54.5 %copy-start.4 = (f32[1024,64]{0,1:T(8,128)S(1)}, f32[1024,64]{0,1:T(8,128)}, u32[]{:S(2)}) copy-start(f32[1024,64]{0,1:T(8,128)} %param.13) | copy-start | bytes 786436
  66.1 20.0 %all-to-all-start.3 = ((f32[64,1,8,512]{3,2,1,0:T(8,128)}), f32[64,1,8,512]{3,2,1,0:T(8,128)S(1)}, u32[]{:S(2)}, u32[]{:S(2)}) async-start(f32[64,1,8,512]{3,2,1,0:T(8,128)} %get-tuple-element.164), calls=%async_computation.3 | async-start | bytes 2097152 | tf_op jit(solution)/shard_map/all_to_all | solution.py:161
  92.0 21.5 %copy-start.2 = (s32[1024,1024]{1,0:T(8,128)}, s32[1024,1024]{1,0:T(8,128)S(1)}, u32[]{:S(2)}) copy-start(s32[1024,1024]{1,0:T(8,128)S(1)} %iota_subtract_fusion.2) | copy-start | bytes 12582916 | tf_op jit(solution)/shard_map/while
  160.5 21.1 %copy-start.2 = (s32[1024,1024]{1,0:T(8,128)}, s32[1024,1024]{1,0:T(8,128)S(1)}, u32[]{:S(2)}) copy-start(s32[1024,1024]{1,0:T(8,128)S(1)} %iota_subtract_fusion.2) | copy-start | bytes 12582916 | tf_op jit(solution)/shard_map/while
  228.6 21.2 %copy-start.2 = (s32[1024,1024]{1,0:T(8,128)}, s32[1024,1024]{1,0:T(8,128)S(1)}, u32[]{:S(2)}) copy-start(s32[1024,1024]{1,0:T(8,128)S(1)} %iota_subtract_fusion.2) | copy-start | bytes 12582916 | tf_op jit(solution)/shard_map/while
  371.5 4.6 copy-start.3
  488.4 126.5 %all-to-all-start.7 = ((f32[64,1,64,512]{3,2,1,0:T(8,128)}), f32[64,1,64,512]{3,2,1,0:T(8,128)}, u32[]{:S(2)}, u32[]{:S(2)}) async-start(f32[64,1,64,512]{3,2,1,0:T(8,128)} %get-tuple-element.161), calls=%async_computation.7 | async-start | bytes 16777216 | tf_op jit(solution)/shard_map/all_to_all | solution.py:187
  614.9 19.5 %copy-start.1 = (f32[48,8,512]{2,1,0:T(8,128)S(1)}, f32[48,8,512]{2,1,0:T(8,128)}, u32[]{:S(2)}) copy-start(f32[48,8,512]{2,1,0:T(8,128)} %param.8) | copy-start | bytes 2359300
where the time goes:
time: 641 us; the launch traced here: 635 us
  blocking collectives  139 us (22%)
  waiting for transfers between devices  134 us (21%)
  matrix products  131 us (20%)
  other arithmetic  110 us (17%)
  local copies, waits for them, and re-layouts  80 us (12%)
  starting transfers between devices  32.7 us (5%)
    all_to_all x1, waiting for transfers between devices, on_device(): lax.all_to_all(back_right, 'cols', split_axis=0, concat_axis=0, tiled=True)  112 us
    all_to_all x1, blocking collectives, on_device(): lax.all_to_all(back_left, 'cols', split_axis=0, concat_axis=0, tiled=True)  103 us
    dot_general x3, matrix products, step(): sketched = jnp.einsum('gik,kr->gir', block, sketch, precision=HIGHEST)  63.7 us
    dot_general x3, matrix products, step(): projected = jnp.einsum('gik,gir->grk', block, sketched, precision=HIGHEST)  62.1 us
    another operation x12, other arithmetic, factor_pair(): lower = jnp.linalg.cholesky(system)  35.7 us
    another operation x9, other arithmetic, factor_pair(): lax.linalg.triangular_solve(lower, half, left_side=True, lower=True, tran...  30.5 us
    all_to_all x1, blocking collectives, on_device(): lax.all_to_all(send_rows, 'cols', split_axis=0, concat_axis=0, tiled=True)  20.9 us
    unnamed x10, local copies, waits for them, and re-layouts  20 us
  transfers between devices with their start and end apart: 4, of which 4 were waited for; matrix products, arithmetic and copies ran while one was open for 2% of the time, Pallas kernels for 0%

commit v1 on v0

v1 whole, which is shorter than its diff:
```python
import functools

import jax
import jax.numpy as jnp
from jax import lax
from jax.experimental import pallas as pl
from jax.experimental.pallas import tpu as pltpu
from jax.sharding import PartitionSpec as P

F32, BF16 = jnp.float32, jnp.bfloat16
GROUP = 8
STRIPE = 256
CHUNK = 128
MESH = pl.DeviceIdType.MESH
ROW_ORDER, COL_ORDER = (0, 0, 1, 1, 0, 2), (0, 1, 0, 1, 2, 0)


def nn(a, b):
    return jnp.dot(a, b, preferred_element_type=F32)


def nt(a, b):
    return lax.dot_general(a, b, (((1,), (1,)), ((), ())), preferred_element_type=F32)


def pieces(x):
    high = x.astype(BF16).astype(F32)
    rest = x - high
    middle = rest.astype(BF16).astype(F32)
    return high, middle, rest - middle


def stacked(x, order):
    parts = pieces(x)
    return jnp.concatenate([parts[k] for k in order], 0).astype(BF16)


def halves(x):
    high = x.astype(BF16)
    return high, (x - high.astype(F32)).astype(BF16)


def row_features(g):
    sub = lax.broadcasted_iota(jnp.int32, g.shape, 0)
    x = [g[k : k + 1] for k in range(3)]
    n = [g[k : k + 1] for k in range(3, 6)]
    p = n[0] * x[0] + n[1] * x[1] + n[2] * x[2]
    sq = x[0] * x[0] + x[1] * x[1] + x[2] * x[2] + (0.1 + 0.05 * g[6:7])
    base = jnp.where(sub < 6, g, jnp.where(sub == 6, 1.0, sq))
    mid = (sub >= 3) & (sub < 6)
    last = base * jnp.where(mid, sq, p)
    return base, jnp.concatenate([base, base * x[0], base * x[1], base * x[2], last], 0)


def col_features(c):
    sub = lax.broadcasted_iota(jnp.int32, c.shape, 0)
    y = [c[k : k + 1] for k in range(3)]
    m = [c[k : k + 1] for k in range(3, 6)]
    q = m[0] * y[0] + m[1] * y[1] + m[2] * y[2]
    area = 0.1 + 0.05 * c[6:7]
    sq = y[0] * y[0] + y[1] * y[1] + y[2] * y[2] + area
    w = -3.0 * area
    mid = (sub >= 3) & (sub < 6)
    up = jnp.where(mid, pltpu.roll(c, 3, 0), 0.0)
    own = jnp.where(mid, area * c, 0.0)
    down = pltpu.roll(c, 5, 0)
    dist = jnp.where(
        sub < 3, -2.0 * c, jnp.where(sub == 6, sq, jnp.where(sub == 7, 1.0, 0.0))
    )
    numer = jnp.concatenate(
        [up * (w * q) + own * sq]
        + [up * (-w * m[b]) - 2.0 * y[b] * own for b in range(3)]
        + [jnp.where(sub < 3, w * down, jnp.where(sub == 6, -w * q, own))],
        0,
    )
    return dist, numer


def block_factors(g, c, delta, live, sk_ref, y_ref, z_ref, fd, fw, ru, rw, bh, bl):
    width, rank = g.shape[1], y_ref.shape[0]
    base, wide = row_features(g)
    ru[...] = stacked(base, ROW_ORDER)
    rw[...] = stacked(wide, ROW_ORDER)
    dist, numer = col_features(c)
    fd[...] = stacked(dist, COL_ORDER).T
    fw[...] = stacked(numer, COL_ORDER).T
    gap = lax.broadcasted_iota(jnp.int32, (CHUNK, STRIPE), 0) - lax.broadcasted_iota(
        jnp.int32, (CHUNK, STRIPE), 1
    )

    def project(prev):
        s, pair, high = prev
        both = nt(pair, bh[s % 2])
        z = both[:rank] + both[rank:] + nt(high, bl[s % 2])
        z_ref[...] = z if s == 0 else z_ref[...] + z

    prev = None
    for s in range(width // STRIPE):
        cols = slice(s * STRIPE, (s + 1) * STRIPE)
        u, w = ru[:, cols], rw[:, cols]
        own = 4.0 + 2.0 * g[7:8, cols]
        for j in range(0, width, CHUNK):
            d = nn(fd[j : j + CHUNK, :], u)
            h = nn(fw[j : j + CHUNK, :], w)
            t = lax.rsqrt(d)
            t2 = t * t
            a = (h * t) * (t2 * t2)
            a = jnp.where(gap == delta + (s * STRIPE - j), own, a)
            high, low = halves(a)
            bh[s % 2, j : j + CHUNK, :] = high
            bl[s % 2, j : j + CHUNK, :] = low
        if prev is not None:
            project(prev)
        both = nn(sk_ref[...], bh[s % 2])
        y = (both[:rank] + both[rank:] + nn(sk_ref[:rank, :], bl[s % 2])) * live
        y_ref[:, cols] = y
        high, low = halves(y)
        prev = (s, jnp.concatenate([high, low], 0), high)
    project(prev)


def system_of(y):
    rank = y.shape[0]
    high, low = halves(y)
    both = nt(jnp.concatenate([high, low], 0), high)
    cross = both[rank:]
    gram = both[:rank] + (cross + cross.T)
    one = (
        lax.broadcasted_iota(jnp.int32, (rank, rank), 0)
        == lax.broadcasted_iota(jnp.int32, (rank, rank), 1)
    ).astype(F32)
    diagonal = jnp.sum(gram * one, axis=0, keepdims=True)
    trace = jnp.sum(diagonal, axis=1, keepdims=True)
    lam = 0.01 * trace / rank + 0.001
    return jnp.concatenate([one, gram + lam * one], 1)


def eliminated(a):
    rank = a.shape[1]
    sub = lax.broadcasted_iota(jnp.int32, (1, rank, 1), 1)
    for k in range(rank):
        row = a[:, k : k + 1, :] * (1.0 / a[:, k : k + 1, rank + k : rank + k + 1])
        a = jnp.where(sub == k, row, a - a[:, :, rank + k : rank + k + 1] * row)
    return a


def times(inverse, z):
    ih, im, il = pieces(inverse)
    zh, zm, zl = pieces(z)
    left = jnp.concatenate([ih, im, ih, im, il, ih], 1).astype(BF16)
    right = jnp.concatenate([zh, zh, zm, zm, zh, zl], 0).astype(BF16)
    return nn(left, right)


def kernel(
    rs_ref, cs_ref, count_ref, row_ref, col_ref, sketch_ref, left_ref, right_ref,
    geo, sk_ref, ybuf, zbuf, mats, fd, fw, ru, rw, bh, bl,
    geo_local, geo_send, geo_recv, out_local, out_send, out_recv,
):
    share, rank, width = ybuf.shape
    half = width // 2
    me = lax.axis_index("rows")
    other = 1 - me

    barrier = pltpu.get_barrier_semaphore()
    pl.semaphore_signal(barrier, inc=1, device_id={"rows": other}, device_id_type=MESH)
    pl.semaphore_wait(barrier, 1)

    mine = pl.ds(pl.multiple_of(me * half, half), half)
    theirs = pl.ds(pl.multiple_of(other * half, half), half)
    moves = []
    for k, ref in enumerate((row_ref, col_ref)):
        moves.append(
            pltpu.make_async_remote_copy(
                src_ref=ref.at[pl.ds(other * share, share)],
                dst_ref=geo.at[k, :, :, mine],
                send_sem=geo_send.at[k],
                recv_sem=geo_recv.at[k],
                device_id={"rows": other},
                device_id_type=MESH,
            )
        )
        moves.append(
            pltpu.make_async_copy(
                ref.at[pl.ds(me * share, share)], geo.at[k, :, :, mine], geo_local.at[k]
            )
        )
    for move in moves:
        move.start()

    s = sketch_ref[...]
    high = s.astype(BF16).astype(F32)
    sk_ref[...] = jnp.concatenate([high, s - high], 1).T.astype(BF16)
    for move in moves:
        move.wait()

    def outgoing(which, buf, out, g):
        blocks = pl.ds(g * GROUP, GROUP)
        places = pl.ds(me * share + g * GROUP, GROUP)
        here = pltpu.make_async_copy(
            buf.at[blocks, :, mine], out.at[places], out_local.at[which, g]
        )
        there = pltpu.make_async_remote_copy(
            src_ref=buf.at[blocks, :, theirs],
            dst_ref=out.at[places],
            send_sem=out_send.at[which, g],
            recv_sem=out_recv.at[which, g],
            device_id={"rows": other},
            device_id_type=MESH,
        )
        return here, there

    def group_step(g, carry):
        def block_step(b, carry):
            k = g * GROUP + b
            place = me * share + k
            delta = rs_ref[place] - cs_ref[place]
            live = jnp.where(place < count_ref[0], 1.0, 0.0)
            block_factors(
                geo[0, k], geo[1, k], delta, live, sk_ref, ybuf.at[k], zbuf.at[k],
                fd, fw, ru, rw, bh, bl,
            )
            mats[b] = system_of(ybuf[k])
            return carry

        lax.fori_loop(0, GROUP, block_step, 0)
        for move in outgoing(0, ybuf, left_ref, g):
            move.start()
        mats[...] = eliminated(mats[...])

        def solve_step(b, carry):
            k = g * GROUP + b
            zbuf[k] = times(mats[b][:, :rank], zbuf[k])
            return carry

        lax.fori_loop(0, GROUP, solve_step, 0)
        for move in outgoing(1, zbuf, right_ref, g):
            move.start()
        return carry

    groups = share // GROUP
    lax.fori_loop(0, groups, group_step, 0)
    for g in range(groups):
        for which, (buf, out) in enumerate(((ybuf, left_ref), (zbuf, right_ref))):
            for move in outgoing(which, buf, out, g):
                move.wait()


def on_device(row_geom, col_geom, row_start, col_start, block_count, sketch):
    owned, geo_count, half = row_geom.shape
    rank = sketch.shape[1]
    share, width = owned // 2, 2 * half
    groups = share // GROUP
    smem = pl.BlockSpec(memory_space=pltpu.SMEM)
    hbm = pl.BlockSpec(memory_space=pl.ANY)
    dma = pltpu.SemaphoreType.DMA
    return pl.pallas_call(
        kernel,
        out_shape=[jax.ShapeDtypeStruct((owned, rank, half), F32)] * 2,
        in_specs=[smem, smem, smem, hbm, hbm, pl.BlockSpec(memory_space=pltpu.VMEM)],
        out_specs=[hbm, hbm],
        scratch_shapes=[
            pltpu.VMEM((2, share, geo_count, width), F32),
            pltpu.VMEM((2 * rank, width), BF16),
            pltpu.VMEM((share, rank, width), F32),
            pltpu.VMEM((share, rank, width), F32),
            pltpu.VMEM((GROUP, rank, 2 * rank), F32),
            pltpu.VMEM((width, 48), BF16),
            pltpu.VMEM((width, 240), BF16),
            pltpu.VMEM((48, width), BF16),
            pltpu.VMEM((240, width), BF16),
            pltpu.VMEM((2, width, STRIPE), BF16),
            pltpu.VMEM((2, width, STRIPE), BF16),
            dma((2,)), dma((2,)), dma((2,)),
            dma((2, groups)), dma((2, groups)), dma((2, groups)),
        ],
        compiler_params=pltpu.CompilerParams(
            collective_id=0, has_side_effects=True, vmem_limit_bytes=48 << 20
        ),
    )(row_start, col_start, block_count, row_geom, col_geom, sketch)


def solution(mesh):
    placed = (
        P("cols", None, "rows"),
        P("cols", None, "rows"),
        P("cols"),
        P("cols"),
        P("cols"),
        P(),
    )
    return jax.shard_map(
        on_device,
        mesh=mesh,
        in_specs=placed,
        out_specs=(P("cols", None, "rows"), P("cols", None, "rows")),
        check_vma=False,
    )
```

time: 641 us -> 142 us (0.22)
  blocking collectives: 139 us -> 0 us
  waiting for transfers between devices: 134 us -> 0 us
  matrix products: 131 us -> 0 us
  Pallas kernels: 0 us -> 125 us
  other arithmetic: 110 us -> 0 us
  local copies, waits for them, and re-layouts: 80 us -> 14.3 us
  starting transfers between devices: 32.7 us -> 0 us
    all_to_all x4 -> x0, blocking collectives: 139 us -> none  [the longest x1 103 us: on_device(): lax.all_to_all(back_left, 'cols', split_axis=0, concat_axis=0, tiled=True)]
    all_to_all x4 -> x0, waiting for transfers between devices: 134 us -> none  [the longest x1 112 us: on_device(): lax.all_to_all(back_right, 'cols', split_axis=0, concat_axis=0, tiled=True)]
    dot_general x9 -> x0, matrix products: 128 us -> none  [the longest x3 63.7 us: step(): sketched = jnp.einsum('gik,kr->gir', block, sketch, precision=HIGHEST)]
    pallas_call x0 -> x1, Pallas kernels: none -> 125 us  [on_device(): pl.pallas_call(kernel, out_shape=[jax.ShapeDtypeStruct((owned, rank, half...]
    another operation x25 -> x0, other arithmetic: 66.3 us -> none  [the longest x12 35.7 us: factor_pair(): lower = jnp.linalg.cholesky(system)]
    all_to_all x4 -> x0, starting transfers between devices: 32.7 us -> none  [the longest x1 11.5 us: copy_for_each(): return lax.all_to_all(copies, axis, split_axis=0, concat_axis=0, tiled=True)]
    gather x12 -> x0, local copies, waits for them, and re-layouts: 32.4 us -> none  [the longest x1 7.11 us: on_device(): right = returned_right.reshape(total_slots, rank, width)[flat_index]]
    select_n x9 -> x0, other arithmetic: 23.1 us -> none  [the longest x1 12.4 us: on_device(): return (jnp.where(is_kept, left, 0.0), jnp.where(is_kept, right, 0.0))]
  transfers between devices with their start and end apart: 4 -> 0, of which waited for: 4 -> 0; matrix products, arithmetic and copies ran while one was open for 2% -> 0% of each run, Pallas kernels for 0% -> 0%
where the time goes in v1:
time: 142 us; the launch traced here: 141 us
  Pallas kernels  125 us (88%)
  local copies, waits for them, and re-layouts  14.3 us (10%)
    pallas_call x1, Pallas kernels, on_device(): pl.pallas_call(kernel, out_shape=[jax.ShapeDtypeStruct((owned, rank, half...  125 us
    unnamed x13, local copies, waits for them, and re-layouts  14.3 us

profile of v1, /device:TPU:4, one launch (start us, length us, event | category | flops | bytes accessed | tf_op | source)
XLA Modules:
  0.0 140.9 jit_solution(10213972161267184835)
XLA Ops:
  1.3 1.1 copy.8.sketch_ref
  2.4 0.0 copy-start
  2.4 1.1 copy-done
  3.6 0.0 copy-start.1
  3.6 1.1 copy-done.1
  4.7 0.0 copy-start.2
  4.7 0.7 copy-done.2
  5.4 0.0 copy-start.3
  5.4 0.7 copy-done.3
  6.0 125.3 %shard_map.77 = (f32[48,64,512]{2,1,0:T(8,128)}, f32[48,64,512]{2,1,0:T(8,128)}) custom-call(s32[48]{0:T(128)S(1)} %copy-done.2, s32[48]{0:T(128)S(1)} %copy-done.3, s32[1]{0:T(128)S(6)} %copy.11.count_ref, f32[48,8,512]{2,1,0:T(8,128)S(1)} %copy-done, f32[48,8,512]{2,1,0:T(8,128)S(1)} %copy-done.1, f32[1024,64]{1,0:T(8,128)S(1)} %copy.8.sketch_ref), custom_call_target="tpu_custom_call" | custom-call | tf_op jit(solution)/shard_map/pallas_call | solution.py:257
  131.3 0.0 copy-start.4
  131.4 6.9 %copy.12 = f32[48,64,512]{2,1,0:T(8,128)} copy(f32[48,64,512]{2,1,0:T(8,128)} %get-tuple-element.4) | data formatting | bytes 12582912
  138.2 0.0 copy-done.4
  138.2 2.7 %copy.13 = f32[48,64,512]{2,1,0:T(8,128)} copy(f32[48,64,512]{2,1,0:T(8,128)S(1)} %copy-done.4) | data formatting | bytes 12582912
Async XLA Ops:
  2.4 1.1 copy-start
  3.6 1.1 copy-start.1
  4.7 0.7 copy-start.2
  5.4 0.7 copy-start.3
  131.3 6.9 %copy-start.4 = (f32[48,64,512]{2,1,0:T(8,128)S(1)}, f32[48,64,512]{2,1,0:T(8,128)}, u32[]{:S(2)}) copy-start(f32[48,64,512]{2,1,0:T(8,128)} %get-tuple-element.5) | copy-start | bytes 18874372

commit v2 on v1

v2 whole, which is shorter than its diff:
```python
import functools

import jax
import jax.numpy as jnp
from jax import lax
from jax.experimental import pallas as pl
from jax.experimental.pallas import tpu as pltpu
from jax.sharding import PartitionSpec as P

F32, BF16 = jnp.float32, jnp.bfloat16
PIVOTS = 2
TOGETHER = 4
STRIPE = 512
CHUNK = 256
MESH = pl.DeviceIdType.MESH
ROW_ORDER, COL_ORDER = (0, 0, 1, 1, 0, 2), (0, 1, 0, 1, 2, 0)


def nn(a, b):
    return jnp.dot(a, b, preferred_element_type=F32)


def nt(a, b):
    return lax.dot_general(a, b, (((1,), (1,)), ((), ())), preferred_element_type=F32)


def pieces(x):
    high = x.astype(BF16).astype(F32)
    rest = x - high
    middle = rest.astype(BF16).astype(F32)
    return high, middle, rest - middle


def stacked(x, order):
    parts = pieces(x)
    return jnp.concatenate([parts[k] for k in order], 0).astype(BF16)


def halves(x):
    high = x.astype(BF16)
    return high, (x - high.astype(F32)).astype(BF16)


def row_features(g):
    sub = lax.broadcasted_iota(jnp.int32, g.shape, 0)
    x = [g[k : k + 1] for k in range(3)]
    n = [g[k : k + 1] for k in range(3, 6)]
    p = n[0] * x[0] + n[1] * x[1] + n[2] * x[2]
    sq = x[0] * x[0] + x[1] * x[1] + x[2] * x[2] + (0.1 + 0.05 * g[6:7])
    base = jnp.where(sub < 6, g, jnp.where(sub == 6, 1.0, sq))
    mid = (sub >= 3) & (sub < 6)
    last = base * jnp.where(mid, sq, p)
    return base, jnp.concatenate([base, base * x[0], base * x[1], base * x[2], last], 0)


def col_features(c):
    sub = lax.broadcasted_iota(jnp.int32, c.shape, 0)
    y = [c[k : k + 1] for k in range(3)]
    m = [c[k : k + 1] for k in range(3, 6)]
    q = m[0] * y[0] + m[1] * y[1] + m[2] * y[2]
    area = 0.1 + 0.05 * c[6:7]
    sq = y[0] * y[0] + y[1] * y[1] + y[2] * y[2] + area
    w = -3.0 * area
    mid = (sub >= 3) & (sub < 6)
    up = jnp.where(mid, pltpu.roll(c, 3, 0), 0.0)
    own = jnp.where(mid, area * c, 0.0)
    down = pltpu.roll(c, 5, 0)
    dist = jnp.where(
        sub < 3, -2.0 * c, jnp.where(sub == 6, sq, jnp.where(sub == 7, 1.0, 0.0))
    )
    numer = jnp.concatenate(
        [up * (w * q) + own * sq]
        + [up * (-w * m[b]) - 2.0 * y[b] * own for b in range(3)]
        + [jnp.where(sub < 3, w * down, jnp.where(sub == 6, -w * q, own))],
        0,
    )
    return dist, numer


def put_features(g, c, fd, fw, ru, rw):
    base, wide = row_features(g)
    ru[...] = stacked(base, ROW_ORDER)
    rw[...] = stacked(wide, ROW_ORDER)
    dist, numer = col_features(c)
    fd[...] = stacked(dist, COL_ORDER).T
    fw[...] = stacked(numer, COL_ORDER).T


def identity(rank):
    return (
        lax.broadcasted_iota(jnp.int32, (rank, rank), 0)
        == lax.broadcasted_iota(jnp.int32, (rank, rank), 1)
    ).astype(F32)


def system_of(products):
    rank = products.shape[1]
    cross = products[rank:]
    gram = products[:rank] + (cross + cross.T)
    one = identity(rank)
    diagonal = jnp.sum(gram * one, axis=0, keepdims=True)
    lam = 0.01 * jnp.sum(diagonal, axis=1, keepdims=True) / rank + 0.001
    return jnp.concatenate([one, gram + lam * one], 1)


def eliminated(a, first, last):
    rank = a.shape[0]
    sub = lax.broadcasted_iota(jnp.int32, (rank, 1), 0)
    for k in range(first, last):
        column = jnp.broadcast_to(a[:, rank + k : rank + k + 1], a.shape)
        row = a[k : k + 1, :] / column[k : k + 1, :]
        a = jnp.where(sub == k, row, a - column * row)
    return a


def times(inverse, z):
    ih, il = halves(inverse)
    zh, zl = halves(z)
    left = jnp.concatenate([inverse_piece.astype(F32) for inverse_piece in (ih, il, ih, il)], 1)
    return nn(left.astype(BF16), jnp.concatenate([zh, zh, zl, zl], 0))


def blocks_step(geo, k, deltas, lives, sk_ref, ybuf, rbuf, zprev, sys_ref, fd, fw, ru, rw, bh, bl):
    rank, width = zprev.shape[1:]
    gap = lax.broadcasted_iota(jnp.int32, (CHUNK, STRIPE), 0) - lax.broadcasted_iota(
        jnp.int32, (CHUNK, STRIPE), 1
    )
    systems = [sys_ref[t] for t in range(TOGETHER)]
    done = 0

    def project(prev):
        slot, pair, high = prev
        both = nt(pair, bh[slot])
        return both[:rank] + both[rank:] + nt(high, bl[slot])

    stripes = width // STRIPE
    finished = []
    for t in range(TOGETHER):
        prev = z = products = None
        for s in range(stripes):
            slot = s % 2
            cols = slice(s * STRIPE, (s + 1) * STRIPE)
            u, w = ru[:, cols], rw[:, cols]
            own = 4.0 + 2.0 * geo[k + t, 0, 7:8, cols]
            for j in range(0, width, CHUNK):
                d = nn(fd[j : j + CHUNK, :], u)
                h = nn(fw[j : j + CHUNK, :], w)
                r = lax.rsqrt(d)
                r2 = r * r
                a = (h * r) * (r2 * r2)
                a = jnp.where(gap == deltas[t] + (s * STRIPE - j), own, a)
                high, low = halves(a)
                bh[slot, j : j + CHUNK, :] = high
                bl[slot, j : j + CHUNK, :] = low
                upto = min(rank, done + PIVOTS)
                systems = [eliminated(a, done, upto) for a in systems]
                done = upto
            if prev is not None:
                part = project(prev)
                z = part if z is None else z + part
            if s == stripes - 1:
                if t == TOGETHER - 1:
                    for b in range(TOGETHER):
                        rbuf[k + b] = times(systems[b][:, :rank], zprev[b])
                put_features(geo[k + t + 1, 0], geo[k + t + 1, 1], fd, fw, ru, rw)
            both = nn(sk_ref[...], bh[slot])
            y = (both[:rank] + both[rank:] + nn(sk_ref[:rank, :], bl[slot])) * lives[t]
            ybuf[k + t, :, cols] = y
            high, low = halves(y)
            pair = jnp.concatenate([high, low], 0)
            part = nt(pair, high)
            products = part if products is None else products + part
            prev = (slot, pair, high)
        finished.append((system_of(products), z + project(prev)))
    for t, (system, z) in enumerate(finished):
        sys_ref[t] = system
        zprev[t] = z


def kernel(
    rs_hbm, cs_hbm, count_hbm, row_ref, col_ref, sketch_ref, left_ref, right_ref,
    geo, sk_ref, ybuf, rbuf, zprev, sys_ref, fd, fw, ru, rw, bh, bl, rs_ref, cs_ref, count_ref,
    small_sem, geo_local, geo_send, geo_recv, out_local, out_send, out_recv,
):
    share, rank, width = ybuf.shape
    half = width // 2
    me = lax.axis_index("rows")
    other = 1 - me

    small = [
        pltpu.make_async_copy(src, dst, small_sem.at[k])
        for k, (src, dst) in enumerate(
            ((rs_hbm, rs_ref), (cs_hbm, cs_ref), (count_hbm, count_ref))
        )
    ]
    for move in small:
        move.start()
    barrier = pltpu.get_barrier_semaphore()
    pl.semaphore_signal(barrier, inc=1, device_id={"rows": other}, device_id_type=MESH)
    pl.semaphore_wait(barrier, 1)

    mine = pl.ds(pl.multiple_of(me * half, half), half)
    theirs = pl.ds(pl.multiple_of(other * half, half), half)
    moves = []
    for k, ref in enumerate((row_ref, col_ref)):
        moves.append(
            pltpu.make_async_remote_copy(
                src_ref=ref.at[pl.ds(other * share, share)],
                dst_ref=geo.at[pl.ds(0, share), k, :, mine],
                send_sem=geo_send.at[k],
                recv_sem=geo_recv.at[k],
                device_id={"rows": other},
                device_id_type=MESH,
            )
        )
        moves.append(
            pltpu.make_async_copy(
                ref.at[pl.ds(me * share, share)],
                geo.at[pl.ds(0, share), k, :, mine],
                geo_local.at[k],
            )
        )
    for move in moves:
        move.start()

    s = sketch_ref[...]
    high = s.astype(BF16).astype(F32)
    sk_ref[...] = jnp.concatenate([high, s - high], 0).astype(BF16)
    for t in range(TOGETHER):
        sys_ref[t] = jnp.concatenate([identity(rank)] * 2, 1)
    zprev[...] = jnp.zeros_like(zprev)
    geo[share] = jnp.zeros(geo.shape[1:], F32)
    for move in small + moves:
        move.wait()
    put_features(geo[0, 0], geo[0, 1], fd, fw, ru, rw)

    def outgoing(which, first, count):
        buf, out, shift = ((ybuf, left_ref, 0), (rbuf, right_ref, TOGETHER))[which]
        blocks = pl.ds(first + shift, count)
        places = pl.ds(me * share + first, count)
        here = pltpu.make_async_copy(
            buf.at[blocks, :, mine], out.at[places], out_local.at[which]
        )
        there = pltpu.make_async_remote_copy(
            src_ref=buf.at[blocks, :, theirs],
            dst_ref=out.at[places],
            send_sem=out_send.at[which],
            recv_sem=out_recv.at[which],
            device_id={"rows": other},
            device_id_type=MESH,
        )
        return here, there

    def step(m, carry):
        k = TOGETHER * m
        places = [me * share + k + t for t in range(TOGETHER)]
        deltas = [rs_ref[p] - cs_ref[p] for p in places]
        lives = [jnp.where(p < count_ref[0], 1.0, 0.0) for p in places]
        blocks_step(
            geo, k, deltas, lives, sk_ref, ybuf, rbuf, zprev, sys_ref, fd, fw, ru, rw, bh, bl
        )
        for move in outgoing(0, k, TOGETHER):
            move.start()

        @pl.when(m > 0)
        def _():
            for move in outgoing(1, k - TOGETHER, TOGETHER):
                move.start()

        return carry

    lax.fori_loop(0, share // TOGETHER, step, 0)
    systems = [eliminated(sys_ref[t], 0, rank) for t in range(TOGETHER)]
    for t in range(TOGETHER):
        rbuf[share + t] = times(systems[t][:, :rank], zprev[t])
    for move in outgoing(1, share - TOGETHER, TOGETHER):
        move.start()
    for which in range(2):
        for move in outgoing(which, 0, share):
            move.wait()


def on_device(row_geom, col_geom, row_start, col_start, block_count, sketch):
    owned, geo_count, half = row_geom.shape
    rank = sketch.shape[1]
    share, width = owned // 2, 2 * half
    hbm = pl.BlockSpec(memory_space=pl.ANY)
    dma = pltpu.SemaphoreType.DMA
    return pl.pallas_call(
        kernel,
        out_shape=[jax.ShapeDtypeStruct((owned, rank, half), F32)] * 2,
        in_specs=[hbm] * 5 + [pl.BlockSpec(memory_space=pltpu.VMEM)],
        out_specs=[hbm, hbm],
        scratch_shapes=[
            pltpu.VMEM((share + 1, 2, geo_count, width), F32),
            pltpu.VMEM((2 * rank, width), BF16),
            pltpu.VMEM((share, rank, width), F32),
            pltpu.VMEM((share + TOGETHER, rank, width), F32),
            pltpu.VMEM((TOGETHER, rank, width), F32),
            pltpu.VMEM((TOGETHER, rank, 2 * rank), F32),
            pltpu.VMEM((width, 48), BF16),
            pltpu.VMEM((width, 240), BF16),
            pltpu.VMEM((48, width), BF16),
            pltpu.VMEM((240, width), BF16),
            pltpu.VMEM((2, width, STRIPE), BF16),
            pltpu.VMEM((2, width, STRIPE), BF16),
            pltpu.SMEM(row_start.shape, jnp.int32),
            pltpu.SMEM(col_start.shape, jnp.int32),
            pltpu.SMEM(block_count.shape, jnp.int32),
            dma((3,)), dma((2,)), dma((2,)), dma((2,)), dma((2,)), dma((2,)), dma((2,)),
        ],
        compiler_params=pltpu.CompilerParams(
            collective_id=0, has_side_effects=True, vmem_limit_bytes=48 << 20
        ),
    )(row_start, col_start, block_count, row_geom, col_geom, sketch.T)


def solution(mesh):
    placed = (
        P("cols", None, "rows"),
        P("cols", None, "rows"),
        P("cols"),
        P("cols"),
        P("cols"),
        P(),
    )
    return jax.shard_map(
        on_device,
        mesh=mesh,
        in_specs=placed,
        out_specs=(P("cols", None, "rows"), P("cols", None, "rows")),
        check_vma=False,
    )
```

time: 142 us -> 118 us (0.83)
  Pallas kernels: 125 us -> 101 us
    pallas_call x1, Pallas kernels: 125 us -> 101 us  [on_device(): pl.pallas_call(kernel, out_shape=[jax.ShapeDtypeStruct((owned, rank, half...]
    unnamed x13 -> x14, local copies, waits for them, and re-layouts: 14.3 us -> 14.1 us
where the time goes in v2:
time: 118 us; the launch traced here: 116 us
  Pallas kernels  101 us (86%)
  local copies, waits for them, and re-layouts  14.1 us (12%)
  between operations  1.31 us (1%)
    pallas_call x1, Pallas kernels, on_device(): pl.pallas_call(kernel, out_shape=[jax.ShapeDtypeStruct((owned, rank, half...  101 us
    unnamed x14, local copies, waits for them, and re-layouts  14.1 us

profile of v2, /device:TPU:4, one launch (start us, length us, event | category | flops | bytes accessed | tf_op | source)
XLA Modules:
  0.0 116.4 jit_solution(7381290855828813321)
XLA Ops:
  1.3 0.0 copy-start
  1.3 1.1 copy-done
  2.4 0.0 copy-start.1
  2.4 1.1 copy-done.1
  3.5 0.0 copy-start.2
  3.5 0.9 copy-done.2
  4.5 0.0 copy-start.3
  4.5 0.7 copy-done.3
  5.2 0.0 copy-start.4
  5.2 0.7 copy-done.4
  5.8 101.0 %shard_map.77 = (f32[48,64,512]{2,1,0:T(8,128)}, f32[48,64,512]{2,1,0:T(8,128)}) custom-call(s32[48]{0:T(128)S(1)} %copy-done.3, s32[48]{0:T(128)S(1)} %copy-done.4, s32[1]{0:T(128)S(6)} %copy.10.count_hbm, f32[48,8,512]{2,1,0:T(8,128)S(1)} %copy-done, f32[48,8,512]{2,1,0:T(8,128)S(1)} %copy-done.1, f32[64,1024]{1,0:T(8,128)S(1)} %bitcast.1), custom_call_target="tpu_custom_call" | custom-call | tf_op jit(solution)/shard_map/pallas_call | solution.py:289
  106.8 0.0 copy-start.5
  106.8 6.9 %copy.11 = f32[48,64,512]{2,1,0:T(8,128)} copy(f32[48,64,512]{2,1,0:T(8,128)} %get-tuple-element.4) | data formatting | bytes 12582912
  113.7 0.0 copy-done.5
  113.7 2.7 %copy.12 = f32[48,64,512]{2,1,0:T(8,128)} copy(f32[48,64,512]{2,1,0:T(8,128)S(1)} %copy-done.5) | data formatting | bytes 12582912
Async XLA Ops:
  1.3 1.1 copy-start
  2.4 1.1 copy-start.1
  3.5 0.9 copy-start.2
  4.5 0.7 copy-start.3
  5.2 0.7 copy-start.4
  106.8 6.9 %copy-start.5 = (f32[48,64,512]{2,1,0:T(8,128)S(1)}, f32[48,64,512]{2,1,0:T(8,128)}, u32[]{:S(2)}) copy-start(f32[48,64,512]{2,1,0:T(8,128)} %get-tuple-element.5) | copy-start | bytes 18874372

commit v3 on v2

--- a/solution.py
+++ b/solution.py
@@ -8,7 +8,7 @@
 from jax.sharding import PartitionSpec as P
 
 F32, BF16 = jnp.float32, jnp.bfloat16
-PIVOTS = 2
+PIVOTS = 3
 TOGETHER = 4
 STRIPE = 512
 CHUNK = 256
@@ -134,11 +134,16 @@
         return both[:rank] + both[rank:] + nt(high, bl[slot])
 
     stripes = width // STRIPE
-    finished = []
+    zs, grams = [None] * TOGETHER, [None] * TOGETHER
+    prev = None
+
+    def add_projection():
+        t, part = prev[0], project(prev[1:])
+        zs[t] = part if zs[t] is None else zs[t] + part
+
     for t in range(TOGETHER):
-        prev = z = products = None
         for s in range(stripes):
-            slot = s % 2
+            slot = (t * stripes + s) % 2
             cols = slice(s * STRIPE, (s + 1) * STRIPE)
             u, w = ru[:, cols], rw[:, cols]
             own = 4.0 + 2.0 * geo[k + t, 0, 7:8, cols]
@@ -153,11 +158,10 @@
                 bh[slot, j : j + CHUNK, :] = high
                 bl[slot, j : j + CHUNK, :] = low
                 upto = min(rank, done + PIVOTS)
-                systems = [eliminated(a, done, upto) for a in systems]
+                systems = [eliminated(m, done, upto) for m in systems]
                 done = upto
             if prev is not None:
-                part = project(prev)
-                z = part if z is None else z + part
+                add_projection()
             if s == stripes - 1:
                 if t == TOGETHER - 1:
                     for b in range(TOGETHER):
@@ -169,12 +173,12 @@
             high, low = halves(y)
             pair = jnp.concatenate([high, low], 0)
             part = nt(pair, high)
-            products = part if products is None else products + part
-            prev = (slot, pair, high)
-        finished.append((system_of(products), z + project(prev)))
-    for t, (system, z) in enumerate(finished):
-        sys_ref[t] = system
-        zprev[t] = z
+            grams[t] = part if grams[t] is None else grams[t] + part
+            prev = (t, slot, pair, high)
+    add_projection()
+    for t in range(TOGETHER):
+        sys_ref[t] = system_of(grams[t])
+        zprev[t] = zs[t]
 
 
 def kernel(
@@ -201,26 +205,31 @@
 
     mine = pl.ds(pl.multiple_of(me * half, half), half)
     theirs = pl.ds(pl.multiple_of(other * half, half), half)
-    moves = []
-    for k, ref in enumerate((row_ref, col_ref)):
-        moves.append(
-            pltpu.make_async_remote_copy(
-                src_ref=ref.at[pl.ds(other * share, share)],
-                dst_ref=geo.at[pl.ds(0, share), k, :, mine],
-                send_sem=geo_send.at[k],
-                recv_sem=geo_recv.at[k],
-                device_id={"rows": other},
-                device_id_type=MESH,
+    def incoming(part, first, count):
+        moves = []
+        for k, ref in enumerate((row_ref, col_ref)):
+            into = geo.at[pl.ds(first, count), k, :, mine]
+            moves.append(
+                pltpu.make_async_remote_copy(
+                    src_ref=ref.at[pl.ds(other * share + first, count)],
+                    dst_ref=into,
+                    send_sem=geo_send.at[part, k],
+                    recv_sem=geo_recv.at[part, k],
+                    device_id={"rows": other},
+                    device_id_type=MESH,
+                )
             )
-        )
-        moves.append(
-            pltpu.make_async_copy(
-                ref.at[pl.ds(me * share, share)],
-                geo.at[pl.ds(0, share), k, :, mine],
-                geo_local.at[k],
+            moves.append(
+                pltpu.make_async_copy(
+                    ref.at[pl.ds(me * share + first, count)], into, geo_local.at[part, k]
+                )
             )
-        )
-    for move in moves:
+        return moves
+
+    early = TOGETHER + 1
+    moves = incoming(0, 0, early)
+    later = incoming(1, early, share - early)
+    for move in moves + later:
         move.start()
 
     s = sketch_ref[...]
@@ -261,6 +270,11 @@
         )
         for move in outgoing(0, k, TOGETHER):
             move.start()
+
+        @pl.when(m == 0)
+        def _():
+            for move in later:
+                move.wait()
 
         @pl.when(m > 0)
         def _():
@@ -307,10 +321,10 @@
             pltpu.SMEM(row_start.shape, jnp.int32),
             pltpu.SMEM(col_start.shape, jnp.int32),
             pltpu.SMEM(block_count.shape, jnp.int32),
-            dma((3,)), dma((2,)), dma((2,)), dma((2,)), dma((2,)), dma((2,)), dma((2,)),
+            dma((3,)), dma((2, 2)), dma((2, 2)), dma((2, 2)), dma((2,)), dma((2,)), dma((2,)),
         ],
         compiler_params=pltpu.CompilerParams(
-            collective_id=0, has_side_effects=True, vmem_limit_bytes=48 << 20
+            collective_id=0, has_side_effects=True, vmem_limit_bytes=62 << 20
         ),
     )(row_start, col_start, block_count, row_geom, col_geom, sketch.T)
 

time: 118 us -> 109 us (0.924)
  Pallas kernels: 101 us -> 96.5 us
  local copies, waits for them, and re-layouts: 14.1 us -> 9.6 us
    unnamed x14 -> x4, local copies, waits for them, and re-layouts: 14.1 us -> 9.6 us
    pallas_call x1, Pallas kernels: 101 us -> 96.5 us  [on_device(): pl.pallas_call(kernel, out_shape=[jax.ShapeDtypeStruct((owned, rank, half...]
where the time goes in v3:
time: 109 us; the launch traced here: 107 us
  Pallas kernels  96.5 us (89%)
  local copies, waits for them, and re-layouts  9.6 us (9%)
  between operations  1.29 us (1%)
    pallas_call x1, Pallas kernels, on_device(): pl.pallas_call(kernel, out_shape=[jax.ShapeDtypeStruct((owned, rank, half...  96.5 us
    unnamed x4, local copies, waits for them, and re-layouts  9.6 us

profile of v3, /device:TPU:4, one launch (start us, length us, event | category | flops | bytes accessed | tf_op | source)
XLA Modules:
  0.0 107.4 jit_solution(16920136060893081994)
XLA Ops:
  1.3 96.5 %shard_map.77 = (f32[48,64,512]{2,1,0:T(8,128)}, f32[48,64,512]{2,1,0:T(8,128)}) custom-call(s32[48]{0:T(128)} %rs_hbm.1, s32[48]{0:T(128)} %cs_hbm.1, s32[1]{0:T(128)S(6)} %copy.10.count_hbm, f32[48,8,512]{2,1,0:T(8,128)} %row_ref.1, f32[48,8,512]{2,1,0:T(8,128)} %col_ref.1, f32[64,1024]{1,0:T(8,128)} %bitcast.1), custom_call_target="tpu_custom_call" | custom-call | tf_op jit(solution)/shard_map/pallas_call | solution.py:303
  97.8 0.0 copy-start
  97.8 6.9 %copy.11 = f32[48,64,512]{2,1,0:T(8,128)} copy(f32[48,64,512]{2,1,0:T(8,128)} %get-tuple-element.4) | data formatting | bytes 12582912
  104.7 0.0 copy-done
  104.7 2.7 %copy.12 = f32[48,64,512]{2,1,0:T(8,128)} copy(f32[48,64,512]{2,1,0:T(8,128)S(1)} %copy-done) | data formatting | bytes 12582912
Async XLA Ops:
  97.8 6.9 %copy-start = (f32[48,64,512]{2,1,0:T(8,128)S(1)}, f32[48,64,512]{2,1,0:T(8,128)}, u32[]{:S(2)}) copy-start(f32[48,64,512]{2,1,0:T(8,128)} %get-tuple-element.5) | copy-start | bytes 18874372
